TPU v7x, 128 devices: a whole 4x4x4 slice. The times are simulated.
128 devices in a mesh: ctx: 32 (over y, x, z_hi), head: 4 (over z_lo, core).
Axes of the slice: x: 4, y: 4, z: 4 (z_hi: 2, z_lo: 2; z = z_hi * 2 + z_lo), core: 2. Of those that a mesh axis runs over, the one named last changes fastest.
Arguments:
- queries: bfloat16 [12288, 8192], P('ctx', 'head'), parts along dimension 1, may hold values from -6 to 6
- key_rows: bfloat16 [12288, 512], P('ctx', 'head'), parts along dimension 1, may hold values from -6 to 6
- value_rows: bfloat16 [12288, 512], P('ctx', 'head'), parts along dimension 1, may hold values from -6 to 6
- out_grad: bfloat16 [12288, 8192], P('ctx', 'head'), parts along dimension 1, may hold values from -6 to 6
- partner: int32 [32, 4], replicated, may hold values from 0 to 31, as said below
- stripes: int32 [96], replicated, may hold values from 0 to 95, each once
Outputs:
- query_grad: bfloat16 [12288, 8192], P('ctx', 'head'), parts along dimension 1
- key_grad: bfloat16 [12288, 512], P('ctx', 'head'), parts along dimension 1
- value_grad: bfloat16 [12288, 512], P('ctx', 'head'), parts along dimension 1
There are 4 independent parts, one for each index of `head`. A program takes and returns all parts, laid end to end along the dimension named above; an argument that names none is the same for every part. Nothing has to cross between parts.
Inputs may be any that keep to these rules, and one draw needn't show every extreme that they name: partner[i, r] = i XOR m_r for 4 distinct nonzero round masks m_r, one of which is 16, so each round pairs the indices of ctx two by two.
All inputs are finite; a program needn't handle non-finite values.
Results may differ from a plain program's by a relative error of at most 0.0064.
Values may be sent and summed in bfloat16 or wider, within the bound.
A program may use at most 256 MiB of HBM per device.

v0:
```python
import functools
import math

import jax
import jax.numpy as jnp
from jax import lax
from jax.experimental import pallas as pl
from jax.experimental.pallas import tpu as pltpu
from jax.sharding import PartitionSpec as P

HEADS = 16
GROUP = 4
WIDTH = 128
BLOCK = 128
OWNED = 3
ROUNDS = 4
ROWS = OWNED * BLOCK
KEY_BLOCKS = OWNED * (ROUNDS + 1)
SCALE = 1.0 / math.sqrt(WIDTH)
SCALE_LOG2 = SCALE * math.log2(math.e)
MESH = pl.DeviceIdType.MESH
F32 = jnp.float32
BF16 = jnp.bfloat16
NT = (((1,), (1,)), ((), ()))


def attend_kernel(
    order_ref, stripes_ref, q_ref, do_ref, kv0, kv1, kv2, kv3, kv4,
    dq_ref, g0, g1, g2, g3, g4,
    kc, vc, kt, bias, s_scr, dp_scr, p_scr, dqt, total, count, order,
):
    kvs = (kv0, kv1, kv2, kv3, kv4)
    grads = (g0, g1, g2, g3, g4)
    a = pl.program_id(0)
    device = lax.axis_index("ctx")
    cols = GROUP * BLOCK
    groups = HEADS // GROUP
    keys = kc.shape[0]

    def place_of(j):
        return stripes_ref[(device ^ order_ref[j // OWNED]) * OWNED + j % OWNED]

    @pl.when(a == 0)
    def _():
        total[...] = jnp.zeros_like(total)
        bias[...] = jnp.zeros_like(bias)
        key = lax.broadcasted_iota(jnp.int32, (BLOCK, BLOCK), 0)
        query = lax.broadcasted_iota(jnp.int32, (BLOCK, BLOCK), 1)
        bias[:BLOCK, :] = jnp.where(key <= query, 0.0, -1e30)

    def block(i):
        return pl.ds(pl.multiple_of(i * BLOCK, BLOCK), BLOCK)

    def put(ref, start, slot):
        src = pl.ds(start, BLOCK)
        k = ref[src, :WIDTH]
        kc[block(slot), :] = k
        vc[block(slot), :] = ref[src, WIDTH:]
        kt[:, block(slot)] = k.T

    place = stripes_ref[device * OWNED + a]
    put(kv0, pl.multiple_of(a * BLOCK, BLOCK), 0)
    order[0] = a
    count[0] = 1
    for j in range(KEY_BLOCKS):
        @pl.when(place_of(j) < place)
        def _():
            slot = count[0]
            put(kvs[j // OWNED], (j % OWNED) * BLOCK, slot)
            order[slot] = j
            count[0] = slot + 1
    n = count[0]
    odd = lax.rem(n, 2) == 1
    chunks = (n + 1) // 2

    @pl.when(odd)
    def _():
        kc[block(n), :] = jnp.zeros((BLOCK, WIDTH), BF16)
        vc[block(n), :] = jnp.zeros((BLOCK, WIDTH), BF16)
        kt[:, block(n)] = jnp.zeros((WIDTH, BLOCK), BF16)
        bias[block(n), :] = jnp.full((BLOCK, BLOCK), -1e30, F32)
        order[n] = KEY_BLOCKS

    def heads(ref, g):
        return jnp.concatenate([ref[:, block(g * GROUP + h)] for h in range(GROUP)], axis=0)

    def fold(x, op):
        return op(x.reshape(x.shape[0] // 8, 8, cols), axis=0)

    def run(first, second, third, top, inverse, delta):
        def chunk(c, carry):
            high, norm, weighted = carry
            rows = pl.ds(pl.multiple_of(c * 256, 256), 256)

            def at(g):
                return pl.ds(pl.multiple_of(lax.rem(g, 2) * keys + c * 256, 256), 256)

            if third is not None:
                p = p_scr[at(third), :] * inverse
                ds = (p * (dp_scr[at(third), :] - delta)).astype(BF16)
                low = p.astype(BF16)
                dk = jnp.dot(ds, heads(q_ref, third), preferred_element_type=F32)
                dv = jnp.dot(low, heads(do_ref, third), preferred_element_type=F32)
                for half in range(2):
                    here, part = block(order[2 * c + half]), slice(half * BLOCK, half * BLOCK + BLOCK)
                    total[here, :WIDTH] += dk[part]
                    total[here, WIDTH:] += dv[part]
                mine = pl.ds(pl.multiple_of(third * cols, cols), cols)
                dqt[:, mine] += jnp.dot(kt[:, rows], ds, preferred_element_type=F32)
            if second is not None:
                p = jnp.exp2((s_scr[at(second), :] - top) * SCALE_LOG2)
                dp = lax.dot_general(vc[rows, :], heads(do_ref, second), NT, preferred_element_type=F32)
                norm += fold(p, jnp.sum)
                weighted += fold(p * dp, jnp.sum)
                p_scr[at(second), :] = p
                dp_scr[at(second), :] = dp
            if first is not None:
                s = lax.dot_general(kc[rows, :], heads(q_ref, first), NT, preferred_element_type=F32)
                s += jnp.concatenate([bias[rows, :]] * GROUP, axis=1)
                high = jnp.maximum(high, fold(s, jnp.max))
                s_scr[at(first), :] = s
            return high, norm, weighted

        zero = jnp.zeros((8, cols), F32)
        high, norm, weighted = lax.fori_loop(0, chunks, chunk, (jnp.full((8, cols), -1e30, F32), zero, zero))
        inverse = 1.0 / jnp.sum(norm, axis=0, keepdims=True)
        return jnp.max(high, axis=0, keepdims=True), inverse, jnp.sum(weighted, axis=0, keepdims=True) * inverse

    dqt[...] = jnp.zeros_like(dqt)
    stats = run(0, None, None, None, None, None)
    stats = run(1, 0, None, stats[0], None, None)
    stats = lax.fori_loop(2, groups, lambda g, stats: run(g, g - 1, g - 2, *stats), stats)
    stats = run(None, groups - 1, groups - 2, *stats)
    run(None, None, groups - 1, *stats)
    for h in range(HEADS):
        here = slice(h * WIDTH, h * WIDTH + WIDTH)
        dq_ref[:, here] = (dqt[:, here] * SCALE).astype(BF16).T

    @pl.when(odd)
    def _():
        bias[block(n), :] = jnp.zeros((BLOCK, BLOCK), F32)

    @pl.when(a == OWNED - 1)
    def _():
        for s in range(ROUNDS + 1):
            rows = slice(s * ROWS, (s + 1) * ROWS)
            grads[s][:, :WIDTH] = (total[rows, :WIDTH] * SCALE).astype(grads[s].dtype)
            grads[s][:, WIDTH:] = total[rows, WIDTH:].astype(grads[s].dtype)


def attend(order, stripes, q, do, kvs):
    smem = pl.BlockSpec(memory_space=pltpu.SMEM)
    part = pl.BlockSpec((ROWS, 2 * WIDTH), lambda a: (0, 0))
    rows = pl.BlockSpec((BLOCK, HEADS * WIDTH), lambda a: (a, 0))
    keys = (KEY_BLOCKS + 1) * BLOCK
    cols = GROUP * BLOCK
    return pl.pallas_call(
        attend_kernel,
        out_shape=[jax.ShapeDtypeStruct(q.shape, BF16), jax.ShapeDtypeStruct((ROWS, 2 * WIDTH), F32)]
        + [jax.ShapeDtypeStruct((ROWS, 2 * WIDTH), BF16)] * ROUNDS,
        grid=(OWNED,),
        in_specs=[smem, smem, rows, rows] + [part] * (ROUNDS + 1),
        out_specs=[rows] + [part] * (ROUNDS + 1),
        scratch_shapes=[
            pltpu.VMEM((keys, WIDTH), BF16),
            pltpu.VMEM((keys, WIDTH), BF16),
            pltpu.VMEM((WIDTH, keys), BF16),
            pltpu.VMEM((keys, BLOCK), F32),
            pltpu.VMEM((2 * keys, cols), F32),
            pltpu.VMEM((2 * keys, cols), F32),
            pltpu.VMEM((2 * keys, cols), F32),
            pltpu.VMEM((WIDTH, HEADS * BLOCK), F32),
            pltpu.VMEM((keys, 2 * WIDTH), F32),
            pltpu.SMEM((1,), jnp.int32),
            pltpu.SMEM((KEY_BLOCKS + 1,), jnp.int32),
        ],
        compiler_params=pltpu.CompilerParams(vmem_limit_bytes=56 * 1024 * 1024),
    )(order, stripes, q, do, *kvs)


FIXED = 16
OTHERS = tuple(m for m in range(1, 32) if m != FIXED)


def plan_kernel(partner_ref, k_ref, v_ref, first_ref, second_ref, third_ref, order_ref, payload_ref):
    payload_ref[:, :WIDTH] = k_ref[...]
    payload_ref[:, WIDTH:] = v_ref[...]
    masks = [partner_ref[r, 0] for r in range(ROUNDS)]
    rest = [jnp.where(masks[r] == FIXED, masks[ROUNDS - 1], masks[r]) for r in range(ROUNDS - 1)]
    for ref, mask in zip((first_ref, second_ref, third_ref), rest):
        ref[0] = jnp.where(mask > FIXED, mask - 2, mask - 1)
    for r, mask in enumerate((0, FIXED, *rest)):
        order_ref[r] = mask


def plan(partner, key_rows, value_rows):
    vmem, smem = pl.BlockSpec(memory_space=pltpu.VMEM), pl.BlockSpec(memory_space=pltpu.SMEM)
    one = jax.ShapeDtypeStruct((1,), jnp.int32)
    return pl.pallas_call(
        plan_kernel,
        out_shape=[one, one, one, jax.ShapeDtypeStruct((ROUNDS + 1,), jnp.int32), jax.ShapeDtypeStruct((ROWS, 2 * WIDTH), BF16)],
        in_specs=[smem, vmem, vmem],
        out_specs=[smem] * 4 + [vmem],
    )(partner.T, key_rows, value_rows)


def finish_kernel(own, p1, p2, p3, p4, dk_ref, dv_ref):
    for ref, cols in ((dk_ref, slice(0, WIDTH)), (dv_ref, slice(WIDTH, 2 * WIDTH))):
        acc = own[:, cols]
        for p in (p1, p2, p3, p4):
            acc += p[:, cols].astype(F32)
        ref[...] = acc.astype(BF16)


def finish(own, parts):
    return pl.pallas_call(finish_kernel, out_shape=[jax.ShapeDtypeStruct((ROWS, WIDTH), BF16)] * 2)(own, *parts)


def swap_kernel(mask, mine, theirs, sent, came):
    partner = {"ctx": lax.axis_index("ctx") ^ mask}
    entered = pltpu.get_barrier_semaphore()
    pl.semaphore_signal(entered, inc=1, device_id=partner, device_id_type=MESH)
    pl.semaphore_wait(entered, 1)
    copy = pltpu.make_async_remote_copy(
        src_ref=mine, dst_ref=theirs, send_sem=sent, recv_sem=came, device_id=partner, device_id_type=MESH
    )
    copy.start()
    copy.wait()


def swap(mask, number, x):
    spec = pl.BlockSpec(memory_space=pl.ANY)
    return pl.pallas_call(
        functools.partial(swap_kernel, mask),
        out_shape=jax.ShapeDtypeStruct(x.shape, x.dtype),
        in_specs=[spec],
        out_specs=spec,
        scratch_shapes=[pltpu.SemaphoreType.DMA, pltpu.SemaphoreType.DMA],
        compiler_params=pltpu.CompilerParams(collective_id=number, has_side_effects=True),
    )(x)


def exchange(branch, arrays):
    fixed, *rest = arrays
    by = [functools.partial(swap, m, i) for i, m in enumerate(OTHERS)]
    across = lax.ppermute(fixed, "ctx", [(i, i ^ FIXED) for i in range(32)])
    return [across, *(lax.switch(b, by, x) for b, x in zip(branch, rest))]


def local(queries, key_rows, value_rows, out_grad, partner, stripes):
    *branch, order, payload = plan(partner, key_rows, value_rows)
    branch = [b.reshape(()) for b in branch]
    kvs = exchange(branch, (payload,) * ROUNDS)
    dq, own, *parts = attend(order, stripes, queries, out_grad, (payload, *kvs))
    return (dq, *finish(own, exchange(branch, parts)))


def solution(mesh):
    return jax.shard_map(
        local,
        mesh=mesh,
        in_specs=(P("ctx", "head"), P("ctx", "head"), P("ctx", "head"), P("ctx", "head"), P(), P()),
        out_specs=(P("ctx", "head"), P("ctx", "head"), P("ctx", "head")),
        check_vma=False,
    )
```

profile of v0, /device:TPU:108, one launch (start us, length us, event | category | flops | bytes accessed | tf_op | source)
XLA Modules:
  0.0 110.3 jit_solution(6615207956600468872)
XLA Ops:
  0.6 1.5 %shard_map.85 = (s32[1]{0:T(128)}, s32[1]{0:T(128)}, s32[1]{0:T(128)}, s32[5]{0:T(128)}, bf16[384,256]{1,0:T(8,128)(2,1)S(1)}) custom-call(s32[4,32]{1,0:T(4,128)} %bitcast.4, bf16[384,128]{1,0:T(8,128)(2,1)} %k_ref.1, bf16[384,128]{1,0:T(8,128)(2,1)} %v_ref.1), custom_call_target="tpu_custom_call" | custom-call | tf_op jit(solution)/shard_map/pallas_call | solution.py:199
  2.2 2.4 %collective-permute-start = (bf16[384,256]{1,0:T(8,128)(2,1)S(1)}, bf16[384,256]{1,0:T(8,128)(2,1)S(1)}, u32[]{:S(2)}, u32[]{:S(2)}) collective-permute-start(bf16[384,256]{1,0:T(8,128)(2,1)S(1)} %get-tuple-element.383.kv0), channel_id=1, source_target_pairs={{0,64},{4,68},{8,72},{12,76},{16,80},{20,84},{24,88},{28,92},{32,9... | collective-permute-start | bytes 589832 | tf_op jit(solution)/shard_map/ppermute | solution.py:246
  6.5 8.1 %conditional.8 = (bf16[384,256]{1,0:T(8,128)(2,1)S(1)}) conditional(s32[]{:T(128)} %bitcast.3, bf16[384,256]{1,0:T(8,128)(2,1)S(1)} %get-tuple-element.383.kv0, bf16[384,256]{1,0:T(8,128)(2,1)S(1)} %get-tuple-element.383.kv0, bf16[384,256]{1,0:T(8,128)(2,1)S(1)} %get-tuple-element.383.kv0, ...), branch_computations={%region_60.0_spmd, %region_61.0_spmd, %region_62.0_spmd, %region_6... | conditional | bytes 8 | solution.py:247
  6.6 8.1 %branch_28_fun.8 = bf16[384,256]{1,0:T(8,128)(2,1)S(1)} custom-call(bf16[384,256]{1,0:T(8,128)(2,1)S(1)} %mine.88), custom_call_target="tpu_custom_call" | custom-call | tf_op jit(solution)/shard_map/cond/branch_28_fun/pallas_call | solution.py:233
  14.6 8.2 %conditional.7 = (bf16[384,256]{1,0:T(8,128)(2,1)S(1)}) conditional(s32[]{:T(128)} %bitcast.2, bf16[384,256]{1,0:T(8,128)(2,1)S(1)} %get-tuple-element.383.kv0, bf16[384,256]{1,0:T(8,128)(2,1)S(1)} %get-tuple-element.383.kv0, bf16[384,256]{1,0:T(8,128)(2,1)S(1)} %get-tuple-element.383.kv0, ...), branch_computations={%region_30.0_spmd, %region_31.0_spmd, %region_32.0_spmd, %region_3... | conditional | bytes 8 | solution.py:247
  14.7 8.2 %branch_16_fun.7 = bf16[384,256]{1,0:T(8,128)(2,1)S(1)} custom-call(bf16[384,256]{1,0:T(8,128)(2,1)S(1)} %mine.46), custom_call_target="tpu_custom_call" | custom-call | tf_op jit(solution)/shard_map/cond/branch_16_fun/pallas_call | solution.py:233
  22.9 6.0 %conditional.6 = (bf16[384,256]{1,0:T(8,128)(2,1)S(1)}) conditional(s32[]{:T(128)} %bitcast.1, bf16[384,256]{1,0:T(8,128)(2,1)S(1)} %get-tuple-element.383.kv0, bf16[384,256]{1,0:T(8,128)(2,1)S(1)} %get-tuple-element.383.kv0, bf16[384,256]{1,0:T(8,128)(2,1)S(1)} %get-tuple-element.383.kv0, ...), branch_computations={%region_0.0_spmd, %region_1.0_spmd, %region_2.0_spmd, %region_3.0_... | conditional | bytes 8 | solution.py:247
  22.9 5.8 %branch_22_fun.6 = bf16[384,256]{1,0:T(8,128)(2,1)S(1)} custom-call(bf16[384,256]{1,0:T(8,128)(2,1)S(1)} %mine.22), custom_call_target="tpu_custom_call" | custom-call | tf_op jit(solution)/shard_map/cond/branch_22_fun/pallas_call | solution.py:233
  28.9 0.0 collective-permute-done.kv1
  28.9 0.0 copy-start
  28.9 0.7 copy-done
  29.6 53.4 %shard_map.86 = (bf16[384,2048]{1,0:T(8,128)(2,1)}, f32[384,256]{1,0:T(8,128)}, bf16[384,256]{1,0:T(8,128)(2,1)}, bf16[384,256]{1,0:T(8,128)(2,1)S(1)}, bf16[384...) custom-call(s32[5]{0:T(128)} %get-tuple-element.382.order_ref, s32[96]{0:T(128)} %stripes_ref.1, ...), custom_call_target="tpu_custom_call" | custom-call | tf_op jit(solution)/shard_map/pallas_call | solution.py:157
  83.0 0.1 collective-permute-start.1
  83.1 8.0 %conditional.9 = (bf16[384,256]{1,0:T(8,128)(2,1)S(1)}) conditional(s32[]{:T(128)} %bitcast.1, bf16[384,256]{1,0:T(8,128)(2,1)S(1)} %get-tuple-element.390, bf16[384,256]{1,0:T(8,128)(2,1)S(1)} %get-tuple-element.390, bf16[384,256]{1,0:T(8,128)(2,1)S(1)} %get-tuple-element.390, ...), branch_computations={%region_90.0_spmd, %region_91.0_spmd, %region_92.0_spmd, %region_9... | conditional | bytes 8 | solution.py:247
  83.1 7.9 %branch_22_fun.9 = bf16[384,256]{1,0:T(8,128)(2,1)S(1)} custom-call(bf16[384,256]{1,0:T(8,128)(2,1)S(1)} %mine.112), custom_call_target="tpu_custom_call" | custom-call | tf_op jit(solution)/shard_map/cond/branch_22_fun/pallas_call | solution.py:233
  91.0 10.1 %conditional.10 = (bf16[384,256]{1,0:T(8,128)(2,1)S(1)}) conditional(s32[]{:T(128)} %bitcast.2, bf16[384,256]{1,0:T(8,128)(2,1)S(1)} %get-tuple-element.391, bf16[384,256]{1,0:T(8,128)(2,1)S(1)} %get-tuple-element.391, bf16[384,256]{1,0:T(8,128)(2,1)S(1)} %get-tuple-element.391, ...), branch_computations={%region_120.0_spmd, %region_121.0_spmd, %region_122.0_spmd, %regio... | conditional | bytes 8 | solution.py:247
  91.1 10.0 %branch_16_fun.10 = bf16[384,256]{1,0:T(8,128)(2,1)S(1)} custom-call(bf16[384,256]{1,0:T(8,128)(2,1)S(1)} %mine.136), custom_call_target="tpu_custom_call" | custom-call | tf_op jit(solution)/shard_map/cond/branch_16_fun/pallas_call | solution.py:233
  101.1 6.7 %conditional.11 = (bf16[384,256]{1,0:T(8,128)(2,1)S(1)}) conditional(s32[]{:T(128)} %bitcast.3, bf16[384,256]{1,0:T(8,128)(2,1)S(1)} %get-tuple-element.392, bf16[384,256]{1,0:T(8,128)(2,1)S(1)} %get-tuple-element.392, bf16[384,256]{1,0:T(8,128)(2,1)S(1)} %get-tuple-element.392, ...), branch_computations={%region_150.0_spmd, %region_151.0_spmd, %region_152.0_spmd, %regio... | conditional | bytes 8 | solution.py:247
  101.2 6.7 %branch_28_fun.11 = bf16[384,256]{1,0:T(8,128)(2,1)S(1)} custom-call(bf16[384,256]{1,0:T(8,128)(2,1)S(1)} %mine.178), custom_call_target="tpu_custom_call" | custom-call | tf_op jit(solution)/shard_map/cond/branch_28_fun/pallas_call | solution.py:233
  107.9 0.0 collective-permute-done.1.p1
  107.9 0.0 copy-start.1
  107.9 0.7 copy-done.1
  108.5 1.8 %shard_map.87 = (bf16[384,128]{1,0:T(8,128)(2,1)}, bf16[384,128]{1,0:T(8,128)(2,1)}) custom-call(f32[384,256]{1,0:T(8,128)} %get-tuple-element.388.own, bf16[384,256]{1,0:T(8,128)(2,1)} %copy-done.1, bf16[384,256]{1,0:T(8,128)(2,1)S(1)} %get-tuple-element.398.p2, bf16[384,256]{1,0:T(8,128)(2,1)S(1)} %get-tuple-element.399.p3, ...), custom_call_target="tpu_custom_call" | custom-call | tf_op jit(solution)/shard_map/pallas_call | solution.py:216
Async XLA Ops:
  2.2 26.8 %collective-permute-start = (bf16[384,256]{1,0:T(8,128)(2,1)S(1)}, bf16[384,256]{1,0:T(8,128)(2,1)S(1)}, u32[]{:S(2)}, u32[]{:S(2)}) collective-permute-start(bf16[384,256]{1,0:T(8,128)(2,1)S(1)} %get-tuple-element.383.kv0), channel_id=1, source_target_pairs={{0,64},{4,68},{8,72},{12,76},{16,80},{20,84},{24,88},{28,92},{32,9... | collective-permute-start | bytes 589832 | tf_op jit(solution)/shard_map/ppermute | solution.py:246
  28.9 0.7 copy-start
  83.0 24.9 %collective-permute-start.1 = (bf16[384,256]{1,0:T(8,128)(2,1)}, bf16[384,256]{1,0:T(8,128)(2,1)S(1)}, u32[]{:S(2)}, u32[]{:S(2)}) collective-permute-start(bf16[384,256]{1,0:T(8,128)(2,1)} %get-tuple-element.389), channel_id=1, source_target_pairs={{0,64},{4,68},{8,72},{12,76},{16,80},{20,84},{24,88},{28,92},{32,9... | collective-permute-start | bytes 589832 | tf_op jit(solution)/shard_map/ppermute | solution.py:246
  107.9 0.7 copy-start.1
where the time goes:
time: 111 us; the launch traced here: 110 us
  Pallas kernels  103 us (93%)
  between operations  2.68 us (2%)
  starting transfers between devices  2.44 us (2%)
  local copies, waits for them, and re-layouts  1.33 us (1%)
    pallas_call x1, Pallas kernels, attend(): pl.pallas_call(attend_kernel, out_shape=[jax.ShapeDtypeStruct(q.shape, BF...  53.4 us
    pallas_call x6, Pallas kernels, swap(): pl.pallas_call(functools.partial(swap_kernel, mask), out_shape=jax.ShapeD...  46.6 us
    ppermute x2, starting transfers between devices, exchange(): across = lax.ppermute(fixed, 'ctx', [(i, i ^ FIXED) for i in range(32)])  2.44 us
  transfers between devices with their start and end apart: 2, of which 0 were waited for; matrix products, arithmetic and copies ran while one was open for 0% of the time, Pallas kernels for 42%

commit v1 on v0

--- a/solution.py
+++ b/solution.py
@@ -9,7 +9,7 @@
 from jax.sharding import PartitionSpec as P
 
 HEADS = 16
-GROUP = 4
+SPLIT = 4
 WIDTH = 128
 BLOCK = 128
 OWNED = 3
@@ -27,15 +27,12 @@
 def attend_kernel(
     order_ref, stripes_ref, q_ref, do_ref, kv0, kv1, kv2, kv3, kv4,
     dq_ref, g0, g1, g2, g3, g4,
-    kc, vc, kt, bias, s_scr, dp_scr, p_scr, dqt, total, count, order,
+    kc, vc, kt, bias, m_scr, dp_scr, p_scr, dqt, qs, dos, total, count, order,
 ):
     kvs = (kv0, kv1, kv2, kv3, kv4)
     grads = (g0, g1, g2, g3, g4)
     a = pl.program_id(0)
     device = lax.axis_index("ctx")
-    cols = GROUP * BLOCK
-    groups = HEADS // GROUP
-    keys = kc.shape[0]
 
     def place_of(j):
         return stripes_ref[(device ^ order_ref[j // OWNED]) * OWNED + j % OWNED]
@@ -81,57 +78,63 @@
         bias[block(n), :] = jnp.full((BLOCK, BLOCK), -1e30, F32)
         order[n] = KEY_BLOCKS
 
-    def heads(ref, g):
-        return jnp.concatenate([ref[:, block(g * GROUP + h)] for h in range(GROUP)], axis=0)
+    for h in range(HEADS):
+        qs[h * BLOCK : (h + 1) * BLOCK, :] = q_ref[:, h * WIDTH : (h + 1) * WIDTH]
+        dos[h * BLOCK : (h + 1) * BLOCK, :] = do_ref[:, h * WIDTH : (h + 1) * WIDTH]
+
+    span = HEADS * BLOCK // SPLIT
+    spans = [slice(i * span, (i + 1) * span) for i in range(SPLIT)]
 
     def fold(x, op):
-        return op(x.reshape(x.shape[0] // 8, 8, cols), axis=0)
-
-    def run(first, second, third, top, inverse, delta):
-        def chunk(c, carry):
-            high, norm, weighted = carry
-            rows = pl.ds(pl.multiple_of(c * 256, 256), 256)
-
-            def at(g):
-                return pl.ds(pl.multiple_of(lax.rem(g, 2) * keys + c * 256, 256), 256)
-
-            if third is not None:
-                p = p_scr[at(third), :] * inverse
-                ds = (p * (dp_scr[at(third), :] - delta)).astype(BF16)
-                low = p.astype(BF16)
-                dk = jnp.dot(ds, heads(q_ref, third), preferred_element_type=F32)
-                dv = jnp.dot(low, heads(do_ref, third), preferred_element_type=F32)
-                for half in range(2):
-                    here, part = block(order[2 * c + half]), slice(half * BLOCK, half * BLOCK + BLOCK)
-                    total[here, :WIDTH] += dk[part]
-                    total[here, WIDTH:] += dv[part]
-                mine = pl.ds(pl.multiple_of(third * cols, cols), cols)
-                dqt[:, mine] += jnp.dot(kt[:, rows], ds, preferred_element_type=F32)
-            if second is not None:
-                p = jnp.exp2((s_scr[at(second), :] - top) * SCALE_LOG2)
-                dp = lax.dot_general(vc[rows, :], heads(do_ref, second), NT, preferred_element_type=F32)
-                norm += fold(p, jnp.sum)
-                weighted += fold(p * dp, jnp.sum)
-                p_scr[at(second), :] = p
-                dp_scr[at(second), :] = dp
-            if first is not None:
-                s = lax.dot_general(kc[rows, :], heads(q_ref, first), NT, preferred_element_type=F32)
-                s += jnp.concatenate([bias[rows, :]] * GROUP, axis=1)
-                high = jnp.maximum(high, fold(s, jnp.max))
-                s_scr[at(first), :] = s
-            return high, norm, weighted
-
-        zero = jnp.zeros((8, cols), F32)
-        high, norm, weighted = lax.fori_loop(0, chunks, chunk, (jnp.full((8, cols), -1e30, F32), zero, zero))
-        inverse = 1.0 / jnp.sum(norm, axis=0, keepdims=True)
-        return jnp.max(high, axis=0, keepdims=True), inverse, jnp.sum(weighted, axis=0, keepdims=True) * inverse
-
+        return op(x.reshape(x.shape[0] // 8, 8, x.shape[1]), axis=0)
+
+    def chunk_rows(c):
+        return pl.ds(pl.multiple_of(c * 256, 256), 256), pl.ds(pl.multiple_of(c * 8, 8), 8)
+
+    def probabilities(c, carry):
+        high, norm, weighted = (list(x) for x in carry)
+        rows, state = chunk_rows(c)
+        mask = bias[rows, :]
+        for i, at in enumerate(spans):
+            s = lax.dot_general(kc[rows, :], qs[at, :], NT, preferred_element_type=F32)
+            s += jnp.concatenate([mask] * (span // BLOCK), axis=1)
+            new = jnp.maximum(high[i], jnp.max(fold(s, jnp.max), axis=0, keepdims=True))
+            p = jnp.exp2((s - new) * SCALE_LOG2)
+            dp = lax.dot_general(vc[rows, :], dos[at, :], NT, preferred_element_type=F32)
+            shrink = jnp.exp2((high[i] - new) * SCALE_LOG2)
+            norm[i] = norm[i] * shrink + fold(p, jnp.sum)
+            weighted[i] = weighted[i] * shrink + fold(p * dp, jnp.sum)
+            high[i] = new
+            m_scr[state, at] = jnp.broadcast_to(new, (8, span))
+            p_scr[rows, at] = p
+            dp_scr[rows, at] = dp
+        return tuple(high), tuple(norm), tuple(weighted)
+
+    zero = (jnp.zeros((8, span), F32),) * SPLIT
+    low = (jnp.full((1, span), -1e30, F32),) * SPLIT
+    high, norm, weighted = lax.fori_loop(0, chunks, probabilities, (low, zero, zero))
+    inverse = [1.0 / jnp.sum(x, axis=0, keepdims=True) for x in norm]
+    delta = [jnp.sum(x, axis=0, keepdims=True) * y for x, y in zip(weighted, inverse)]
     dqt[...] = jnp.zeros_like(dqt)
-    stats = run(0, None, None, None, None, None)
-    stats = run(1, 0, None, stats[0], None, None)
-    stats = lax.fori_loop(2, groups, lambda g, stats: run(g, g - 1, g - 2, *stats), stats)
-    stats = run(None, groups - 1, groups - 2, *stats)
-    run(None, None, groups - 1, *stats)
+
+    def products(c, _):
+        rows, state = chunk_rows(c)
+        dk = dv = None
+        for i, at in enumerate(spans):
+            factor = jnp.exp2((m_scr[state, at][:1] - high[i]) * SCALE_LOG2) * inverse[i]
+            p = p_scr[rows, at] * factor
+            ds = (p * (dp_scr[rows, at] - delta[i])).astype(BF16)
+            dk_part = jnp.dot(ds, qs[at, :], preferred_element_type=F32)
+            dv_part = jnp.dot(p.astype(BF16), dos[at, :], preferred_element_type=F32)
+            dk, dv = (dk_part, dv_part) if dk is None else (dk + dk_part, dv + dv_part)
+            dqt[:, at] += jnp.dot(kt[:, rows], ds, preferred_element_type=F32)
+        for half in range(2):
+            here, part = block(order[2 * c + half]), slice(half * BLOCK, half * BLOCK + BLOCK)
+            total[here, :WIDTH] += dk[part]
+            total[here, WIDTH:] += dv[part]
+        return 0
+
+    lax.fori_loop(0, chunks, products, 0)
     for h in range(HEADS):
         here = slice(h * WIDTH, h * WIDTH + WIDTH)
         dq_ref[:, here] = (dqt[:, here] * SCALE).astype(BF16).T
@@ -153,7 +156,7 @@
     part = pl.BlockSpec((ROWS, 2 * WIDTH), lambda a: (0, 0))
     rows = pl.BlockSpec((BLOCK, HEADS * WIDTH), lambda a: (a, 0))
     keys = (KEY_BLOCKS + 1) * BLOCK
-    cols = GROUP * BLOCK
+    cols = HEADS * BLOCK
     return pl.pallas_call(
         attend_kernel,
         out_shape=[jax.ShapeDtypeStruct(q.shape, BF16), jax.ShapeDtypeStruct((ROWS, 2 * WIDTH), F32)]
@@ -166,10 +169,12 @@
             pltpu.VMEM((keys, WIDTH), BF16),
             pltpu.VMEM((WIDTH, keys), BF16),
             pltpu.VMEM((keys, BLOCK), F32),
-            pltpu.VMEM((2 * keys, cols), F32),
-            pltpu.VMEM((2 * keys, cols), F32),
-            pltpu.VMEM((2 * keys, cols), F32),
+            pltpu.VMEM(((KEY_BLOCKS + 1) // 2 * 8, cols), F32),
+            pltpu.VMEM((keys, cols), F32),
+            pltpu.VMEM((keys, cols), F32),
             pltpu.VMEM((WIDTH, HEADS * BLOCK), F32),
+            pltpu.VMEM((HEADS * BLOCK, WIDTH), BF16),
+            pltpu.VMEM((HEADS * BLOCK, WIDTH), BF16),
             pltpu.VMEM((keys, 2 * WIDTH), F32),
             pltpu.SMEM((1,), jnp.int32),
             pltpu.SMEM((KEY_BLOCKS + 1,), jnp.int32),

time: 111 us -> 113 us (1.018)
  the two profiles are of different devices: /device:TPU:108 before, /device:TPU:0 now
where the time goes in v1:
time: 113 us; the launch traced here: 112 us
  Pallas kernels  104 us (92%)
  starting transfers between devices  3.42 us (3%)
  between operations  2.68 us (2%)
  local copies, waits for them, and re-layouts  1.33 us (1%)
    pallas_call x6, Pallas kernels, swap(): pl.pallas_call(functools.partial(swap_kernel, mask), out_shape=jax.ShapeD...  69.2 us
    pallas_call x1, Pallas kernels, attend(): pl.pallas_call(attend_kernel, out_shape=[jax.ShapeDtypeStruct(q.shape, BF...  31.7 us
    ppermute x2, starting transfers between devices, exchange(): across = lax.ppermute(fixed, 'ctx', [(i, i ^ FIXED) for i in range(32)])  3.42 us
  transfers between devices with their start and end apart: 2, of which 0 were waited for; matrix products, arithmetic and copies ran while one was open for 0% of the time, Pallas kernels for 62%

profile of v1, /device:TPU:0, one launch (start us, length us, event | category | flops | bytes accessed | tf_op | source)
XLA Modules:
  0.0 112.3 jit_solution(11670583522823353364)
XLA Ops:
  0.6 1.5 %shard_map.85 = (s32[1]{0:T(128)}, s32[1]{0:T(128)}, s32[1]{0:T(128)}, s32[5]{0:T(128)}, bf16[384,256]{1,0:T(8,128)(2,1)S(1)}) custom-call(s32[4,32]{1,0:T(4,128)} %bitcast.4, bf16[384,128]{1,0:T(8,128)(2,1)} %k_ref.1, bf16[384,128]{1,0:T(8,128)(2,1)} %v_ref.1), custom_call_target="tpu_custom_call" | custom-call | tf_op jit(solution)/shard_map/pallas_call | solution.py:204
  2.2 3.4 %collective-permute-start = (bf16[384,256]{1,0:T(8,128)(2,1)S(1)}, bf16[384,256]{1,0:T(8,128)(2,1)S(1)}, u32[]{:S(2)}, u32[]{:S(2)}) collective-permute-start(bf16[384,256]{1,0:T(8,128)(2,1)S(1)} %get-tuple-element.383.kv0), channel_id=1, source_target_pairs={{0,64},{4,68},{8,72},{12,76},{16,80},{20,84},{24,88},{28,92},{32,9... | collective-permute-start | bytes 589832 | tf_op jit(solution)/shard_map/ppermute | solution.py:251
  7.5 12.3 %conditional.8 = (bf16[384,256]{1,0:T(8,128)(2,1)S(1)}) conditional(s32[]{:T(128)} %bitcast.3, bf16[384,256]{1,0:T(8,128)(2,1)S(1)} %get-tuple-element.383.kv0, bf16[384,256]{1,0:T(8,128)(2,1)S(1)} %get-tuple-element.383.kv0, bf16[384,256]{1,0:T(8,128)(2,1)S(1)} %get-tuple-element.383.kv0, ...), branch_computations={%region_60.0_spmd, %region_61.0_spmd, %region_62.0_spmd, %region_6... | conditional | bytes 8 | solution.py:252
  7.5 12.2 %branch_29_fun.8 = bf16[384,256]{1,0:T(8,128)(2,1)S(1)} custom-call(bf16[384,256]{1,0:T(8,128)(2,1)S(1)} %mine.89), custom_call_target="tpu_custom_call" | custom-call | tf_op jit(solution)/shard_map/cond/branch_29_fun/pallas_call | solution.py:238
  19.7 8.2 %conditional.7 = (bf16[384,256]{1,0:T(8,128)(2,1)S(1)}) conditional(s32[]{:T(128)} %bitcast.2, bf16[384,256]{1,0:T(8,128)(2,1)S(1)} %get-tuple-element.383.kv0, bf16[384,256]{1,0:T(8,128)(2,1)S(1)} %get-tuple-element.383.kv0, bf16[384,256]{1,0:T(8,128)(2,1)S(1)} %get-tuple-element.383.kv0, ...), branch_computations={%region_30.0_spmd, %region_31.0_spmd, %region_32.0_spmd, %region_3... | conditional | bytes 8 | solution.py:252
  19.8 8.2 %branch_2_fun.7 = bf16[384,256]{1,0:T(8,128)(2,1)S(1)} custom-call(bf16[384,256]{1,0:T(8,128)(2,1)S(1)} %mine.32), custom_call_target="tpu_custom_call" | custom-call | tf_op jit(solution)/shard_map/cond/branch_2_fun/pallas_call | solution.py:238
  28.0 9.6 %conditional.6 = (bf16[384,256]{1,0:T(8,128)(2,1)S(1)}) conditional(s32[]{:T(128)} %bitcast.1, bf16[384,256]{1,0:T(8,128)(2,1)S(1)} %get-tuple-element.383.kv0, bf16[384,256]{1,0:T(8,128)(2,1)S(1)} %get-tuple-element.383.kv0, bf16[384,256]{1,0:T(8,128)(2,1)S(1)} %get-tuple-element.383.kv0, ...), branch_computations={%region_0.0_spmd, %region_1.0_spmd, %region_2.0_spmd, %region_3.0_... | conditional | bytes 8 | solution.py:252
  28.1 9.4 %branch_20_fun.6 = bf16[384,256]{1,0:T(8,128)(2,1)S(1)} custom-call(bf16[384,256]{1,0:T(8,128)(2,1)S(1)} %mine.20), custom_call_target="tpu_custom_call" | custom-call | tf_op jit(solution)/shard_map/cond/branch_20_fun/pallas_call | solution.py:238
  37.6 0.0 collective-permute-done.kv1
  37.7 0.0 copy-start
  37.7 0.7 copy-done
  38.3 31.7 %shard_map.86 = (bf16[384,2048]{1,0:T(8,128)(2,1)}, f32[384,256]{1,0:T(8,128)}, bf16[384,256]{1,0:T(8,128)(2,1)}, bf16[384,256]{1,0:T(8,128)(2,1)S(1)}, bf16[384...) custom-call(s32[5]{0:T(128)} %get-tuple-element.382.order_ref, s32[96]{0:T(128)} %stripes_ref.1, ...), custom_call_target="tpu_custom_call" | custom-call | tf_op jit(solution)/shard_map/pallas_call | solution.py:160
  70.0 0.1 collective-permute-start.1
  70.1 9.5 %conditional.9 = (bf16[384,256]{1,0:T(8,128)(2,1)S(1)}) conditional(s32[]{:T(128)} %bitcast.1, bf16[384,256]{1,0:T(8,128)(2,1)S(1)} %get-tuple-element.390, bf16[384,256]{1,0:T(8,128)(2,1)S(1)} %get-tuple-element.390, bf16[384,256]{1,0:T(8,128)(2,1)S(1)} %get-tuple-element.390, ...), branch_computations={%region_90.0_spmd, %region_91.0_spmd, %region_92.0_spmd, %region_9... | conditional | bytes 8 | solution.py:252
  70.1 9.4 %branch_20_fun.9 = bf16[384,256]{1,0:T(8,128)(2,1)S(1)} custom-call(bf16[384,256]{1,0:T(8,128)(2,1)S(1)} %mine.110), custom_call_target="tpu_custom_call" | custom-call | tf_op jit(solution)/shard_map/cond/branch_20_fun/pallas_call | solution.py:238
  79.6 18.6 %conditional.10 = (bf16[384,256]{1,0:T(8,128)(2,1)S(1)}) conditional(s32[]{:T(128)} %bitcast.2, bf16[384,256]{1,0:T(8,128)(2,1)S(1)} %get-tuple-element.391, bf16[384,256]{1,0:T(8,128)(2,1)S(1)} %get-tuple-element.391, bf16[384,256]{1,0:T(8,128)(2,1)S(1)} %get-tuple-element.391, ...), branch_computations={%region_120.0_spmd, %region_121.0_spmd, %region_122.0_spmd, %regio... | conditional | bytes 8 | solution.py:252
  79.6 18.6 %branch_2_fun.10 = bf16[384,256]{1,0:T(8,128)(2,1)S(1)} custom-call(bf16[384,256]{1,0:T(8,128)(2,1)S(1)} %mine.122), custom_call_target="tpu_custom_call" | custom-call | tf_op jit(solution)/shard_map/cond/branch_2_fun/pallas_call | solution.py:238
  98.2 11.6 %conditional.11 = (bf16[384,256]{1,0:T(8,128)(2,1)S(1)}) conditional(s32[]{:T(128)} %bitcast.3, bf16[384,256]{1,0:T(8,128)(2,1)S(1)} %get-tuple-element.392, bf16[384,256]{1,0:T(8,128)(2,1)S(1)} %get-tuple-element.392, bf16[384,256]{1,0:T(8,128)(2,1)S(1)} %get-tuple-element.392, ...), branch_computations={%region_150.0_spmd, %region_151.0_spmd, %region_152.0_spmd, %regio... | conditional | bytes 8 | solution.py:252
  98.3 11.5 %branch_29_fun.11 = bf16[384,256]{1,0:T(8,128)(2,1)S(1)} custom-call(bf16[384,256]{1,0:T(8,128)(2,1)S(1)} %mine.179), custom_call_target="tpu_custom_call" | custom-call | tf_op jit(solution)/shard_map/cond/branch_29_fun/pallas_call | solution.py:238
  109.8 0.0 collective-permute-done.1.p1
  109.8 0.0 copy-start.1
  109.8 0.7 copy-done.1
  110.5 1.8 %shard_map.87 = (bf16[384,128]{1,0:T(8,128)(2,1)}, bf16[384,128]{1,0:T(8,128)(2,1)}) custom-call(f32[384,256]{1,0:T(8,128)} %get-tuple-element.388.own, bf16[384,256]{1,0:T(8,128)(2,1)} %copy-done.1, bf16[384,256]{1,0:T(8,128)(2,1)S(1)} %get-tuple-element.398.p2, bf16[384,256]{1,0:T(8,128)(2,1)S(1)} %get-tuple-element.399.p3, ...), custom_call_target="tpu_custom_call" | custom-call | tf_op jit(solution)/shard_map/pallas_call | solution.py:221
Async XLA Ops:
  2.2 35.5 %collective-permute-start = (bf16[384,256]{1,0:T(8,128)(2,1)S(1)}, bf16[384,256]{1,0:T(8,128)(2,1)S(1)}, u32[]{:S(2)}, u32[]{:S(2)}) collective-permute-start(bf16[384,256]{1,0:T(8,128)(2,1)S(1)} %get-tuple-element.383.kv0), channel_id=1, source_target_pairs={{0,64},{4,68},{8,72},{12,76},{16,80},{20,84},{24,88},{28,92},{32,9... | collective-permute-start | bytes 589832 | tf_op jit(solution)/shard_map/ppermute | solution.py:251
  37.7 0.7 copy-start
  70.0 39.8 %collective-permute-start.1 = (bf16[384,256]{1,0:T(8,128)(2,1)}, bf16[384,256]{1,0:T(8,128)(2,1)S(1)}, u32[]{:S(2)}, u32[]{:S(2)}) collective-permute-start(bf16[384,256]{1,0:T(8,128)(2,1)} %get-tuple-element.389), channel_id=1, source_target_pairs={{0,64},{4,68},{8,72},{12,76},{16,80},{20,84},{24,88},{28,92},{32,9... | collective-permute-start | bytes 589832 | tf_op jit(solution)/shard_map/ppermute | solution.py:251
  109.8 0.7 copy-start.1
